TPU v7x, 32 devices: a whole 2x2x4 slice. The times are simulated.
32 devices in a mesh: section: 4 (over y, x), grp: 4 (over z), cent: 2 (over core).
Axes of the slice: x: 2, y: 2, z: 4, core: 2. Of those that a mesh axis runs over, the one named last changes fastest.
Arguments:
- latents: bfloat16 [768, 1024], P(('section', 'grp', 'cent')), may hold values from -27 to 27
- valid_mask: int32 [768], P(('section', 'grp', 'cent')), may hold values from 0 to 1, as said below
- centroids: float32 [65536, 1024], P(('section', 'cent')), may hold values from -12 to 12
Outputs:
- refreshed: float32 [65536, 1024], P(('section', 'cent'))
Inputs may be any that keep to these rules, and one draw needn't show every extreme that they name: `valid_mask`: each device's block of 24 frames has its valid frames first; a block has at least 6 and at most 18 valid frames, and some block has exactly 18.
All inputs are finite; a program needn't handle non-finite values.
Results may differ from a plain program's by a relative error of at most 0.0044.
Values may be sent and summed in bfloat16 or wider, within the bound.
No kernel may reach another device: no remote copies, remote signals or barrier semaphores. Data moves between devices by JAX's collectives and lax.ppermute only.
A program may use at most 192 MiB of HBM per device.

v0:
```python
import math

import jax
import jax.numpy as jnp
from jax import lax
from jax.sharding import PartitionSpec as P

W = 1024
VMAX = 18


prior_weight = 0.05


def per_device(latents, valid_mask, centroids):
    frame_rows, frame_flags = (
        lax.all_gather(latents[:VMAX], ("section", "cent"), axis=0, tiled=True),
        lax.all_gather(valid_mask[:VMAX], ("section", "cent"), axis=0, tiled=True),
    )
    inverse_temp = 3.0 / math.sqrt(W)
    cent_low = centroids.astype(jnp.bfloat16)
    scores = (
        lax.dot_general(
            frame_rows, cent_low, (((1,), (1,)), ((), ())), preferred_element_type=jnp.float32
        )
        * inverse_temp
    )
    local_max = jnp.max(scores, axis=1)
    row_max = lax.pmax(local_max, ("section", "cent"))
    row_total = lax.psum(jnp.sum(jnp.exp(scores - row_max[:, None]), axis=1), ("section", "cent"))
    keep_mask = frame_flags.astype(jnp.float32)
    weights = (keep_mask[:, None] * jnp.exp(scores - row_max[:, None]) / row_total[:, None]).astype(
        jnp.bfloat16
    )
    center_sums = lax.dot_general(
        weights, frame_rows, (((0,), (0,)), ((), ())), preferred_element_type=jnp.float32
    )
    soft_counts = jnp.sum(weights, axis=0, dtype=jnp.float32)
    total_sums, total_counts = lax.psum((center_sums, soft_counts), "grp")
    return (total_sums + prior_weight * centroids) / (total_counts + prior_weight)[:, None]


def solution(mesh):
    in_specs = (
        P(("section", "grp", "cent"), None),
        P(("section", "grp", "cent")),
        P(("section", "cent"), None),
    )
    out_specs = P(("section", "cent"), None)
    return jax.shard_map(
        per_device, mesh=mesh, in_specs=in_specs, out_specs=out_specs, check_vma=False
    )
```

profile of v0, /device:TPU:0, one launch (start us, length us, event | category | flops | bytes accessed | tf_op | source)
XLA Modules:
  0.0 1234.0 jit_solution(9228132825352176027)
XLA Ops:
  6.5 0.0 all-reduce.3.cloned.1.call-start
  6.5 1.2 dynamic-slice
  8.4 0.8 slice_dynamic-update-slice_fusion
  9.2 9.5 all-reduce
  18.7 0.8 slice_bitcast_fusion
  19.5 8.9 all-gather
  28.4 0.1 reshape.8
  28.5 15.7 %fusion.6 = (f32[144]{0:T(256)S(1)}, f32[144,8192]{1,0:T(8,128)}) fusion(bf16[144,1024]{1,0:T(8,128)(2,1)S(1)} %reshape.8, f32[8192,1024]{1,0:T(8,128)} %param.5), kind=kOutput, calls=%fused_computation.11 | convolution fusion | flops 2426666752 | bytes 38568512 | tf_op jit(solution)/shard_map/dot_general | solution.py:23
  44.2 13.2 %pmax.7 = f32[144]{0:T(256)S(1)} all-reduce(f32[144]{0:T(256)S(1)} %get-tuple-element.7), channel_id=1, replica_groups=mesh['section'=4,'grp'=4,'cent'=2] {'section','cent'}, use_global_device_ids=true, to_apply=%region_1.0 | all-reduce | flops 144 | bytes 1152 | tf_op jit(solution)/shard_map/pmax | solution.py:29
  57.4 3.1 fusion.5
  60.5 11.8 psum.21
  72.3 3.5 convert_reduce_fusion
  75.8 14.1 %fusion.7 = f32[8192,1024]{1,0:T(8,128)} fusion(bf16[144,8192]{1,0:T(8,128)(2,1)S(1)} %get-tuple-element.6, bf16[144,1024]{1,0:T(8,128)(2,1)S(1)} %reshape.8), kind=kOutput, calls=%fused_computation.12 | convolution fusion | flops 2415919104 | bytes 36208640 | tf_op jit(solution)/shard_map/dot_general | solution.py:35
  90.0 0.0 all-reduce.3.cloned.1.call-update
  90.0 21.6 %psum.23 = f32[8192]{0:T(1024)S(1)} all-reduce(f32[8192]{0:T(1024)S(1)} %get-tuple-element.5), channel_id=1, replica_groups=mesh['section'=4,'grp'=4,'cent'=2] {'grp'}, use_global_device_ids=true, to_apply=%region_6.0 | all-reduce | flops 8192 | bytes 65536 | tf_op jit(solution)/shard_map/psum | solution.py:39
  111.6 1082.7 %all-reduce.3.cloned.1.call-done = f32[8192,1024]{1,0:T(8,128)} async-done(((f32[8192,1024]{1,0:T(8,128)}), f32[8192,1024]{1,0:T(8,128)}) %all-reduce.3.cloned.1.call-update) | async-done | bytes 33554448 | tf_op jit(solution)/shard_map/psum | solution.py:39
  1194.3 32.9 %add_divide_fusion = f32[8192,1024]{1,0:T(8,128)} fusion(f32[8192,1024]{1,0:T(8,128)} %all-reduce.3.cloned.1.call-done, f32[8192,1024]{1,0:T(8,128)} %param.5, f32[8192]{0:T(1024)S(1)} %broadcast_add_fusion), kind=kLoop, calls=%fused_computation | loop fusion | flops 25165824 | bytes 100696064 | tf_op jit(solution)/shard_map/div | solution.py:40
  (3 shorter events, 0.0 us)
Async XLA Ops:
  6.5 1187.7 %all-reduce.3.cloned.1.call-start = ((), (), s32[]{:S(2)}) async-start(), calls=%async_computation | async-start | bytes 67108864 | tf_op jit(solution)/shard_map/psum | solution.py:39
Sparse Core Ops, SparseCore 0:
  90.1 1104.1 all-reduce.2
where the time goes:
time: 1230 us
  waiting for transfers between devices  1080 us (88%)
  blocking collectives  65 us (5%)
  other arithmetic  39.5 us (3%)
  matrix products  29.9 us (2%)
  between operations  14.1 us (1%)
    psum x1, waiting for transfers between devices, per_device(): total_sums, total_counts = lax.psum((center_sums, soft_counts), 'grp')  1080 us
    div x1, other arithmetic, per_device(): (total_sums + prior_weight * centroids) / (total_counts + prior_weight)[:...  32.9 us
  transfers between devices with their start and end apart: 1, of which 1 were waited for; matrix products, arithmetic and copies ran while one was open for 0% of the time, Pallas kernels for 0%

commit v1 on v0

v1 whole, which is shorter than its diff:
```python
import functools
import math

import jax
import jax.numpy as jnp
from jax import lax
from jax.experimental import pallas as pl
from jax.experimental.pallas import tpu as pltpu
from jax.sharding import PartitionSpec as P

VMAX = 18
LANES = 128
ROWS = 16
f32, bf16 = jnp.float32, jnp.bfloat16

prior_weight = 0.05


def pack_body(axes, lat_ref, mask_ref, out_ref):
    width = lat_ref.shape[1]
    rows = lat_ref[...].astype(f32)
    fold = width // LANES
    pieces = [
        rows[r : r + 1, j * LANES : (j + 1) * LANES] for r in range(ROWS, VMAX) for j in range(fold)
    ]
    count = jnp.sum(mask_ref[...].astype(f32), axis=1, keepdims=True)
    block = jnp.int32(0)
    for name, size in axes:
        block = block * size + lax.axis_index(name)
    lane = lax.broadcasted_iota(jnp.int32, (ROWS, LANES), 1)
    tail = jnp.where(lane == 0, count, jnp.where(lane == 1, block.astype(f32), 0.0))
    out_ref[:, :width] = rows[:ROWS].astype(bf16)
    out_ref[:, width : width + LANES] = jnp.concatenate(pieces, axis=0).astype(bf16)
    out_ref[:, width + LANES :] = tail.astype(bf16)


def scores_body(k, cb, sizes, c_ref, *refs):
    n_in = len(refs) - 8
    packed = refs[:n_in]
    fr_ref, e_ref, mb_ref, st_ref, n_ref, all_ref, ext_ref, meta_ref = refs[n_in:]
    cents, width = c_ref.shape
    frames = fr_ref.shape[0]
    steps = cents // cb

    at = 0
    for part in packed:
        for i in range(part.shape[0]):
            all_ref[at : at + ROWS, :] = part[i, :, :width]
            ext_ref[at : at + ROWS, :] = part[i, :, width : width + LANES].astype(f32)
            meta_ref[at : at + ROWS, :] = part[i, :, width + LANES :].astype(f32)
            at += ROWS
    blocks = at // ROWS
    meta = meta_ref[pl.ds(0, blocks, stride=ROWS), :]
    count, number = meta[:, 0:1], meta[:, 1:2]
    total = jnp.sum(count)
    n_ref[0] = total.astype(jnp.int32)

    def place(rows, block_of, row_of):
        block = lax.broadcasted_iota(jnp.int32, (blocks, rows), 0)
        r = lax.broadcasted_iota(jnp.int32, (blocks, rows), 1)
        mine = block == block_of(r)
        length = jnp.sum(jnp.where(mine, count, 0.0), axis=0, keepdims=True)
        own = jnp.sum(jnp.where(mine, number, 0.0), axis=0, keepdims=True)
        before = jnp.sum(jnp.where(number < own, count, 0.0), axis=0, keepdims=True)
        row = row_of(lax.broadcasted_iota(jnp.int32, (1, rows), 1)).astype(f32)
        return jnp.where(row < length, before + row, -1.0)

    def one_hot(to):
        p = lax.broadcasted_iota(jnp.int32, (frames, to.shape[1]), 0).astype(f32)
        return jnp.where(p == to, 1.0, 0.0).astype(bf16)

    extra = VMAX - ROWS
    fold = width // LANES
    main_to = place(at, lambda r: r // ROWS, lambda r: r % ROWS)
    extra_to = place(extra * blocks, lambda r: r % blocks, lambda r: ROWS + r // blocks)
    extra_rows = jnp.concatenate(
        [
            jnp.concatenate(
                [ext_ref[pl.ds(r * fold + j, blocks, stride=ROWS), :] for j in range(fold)], axis=1
            )
            for r in range(extra)
        ],
        axis=0,
    ).astype(bf16)
    ordered = lax.dot_general(
        one_hot(main_to), all_ref[...], (((1,), (0,)), ((), ())), preferred_element_type=f32
    ) + lax.dot_general(
        one_hot(extra_to), extra_rows, (((1,), (0,)), ((), ())), preferred_element_type=f32
    )
    fr_ref[...] = ordered.astype(bf16)

    def run(size):
        st_ref[...] = jnp.zeros_like(st_ref)

        def step(b, carry):
            top, tot = carry
            rows = pl.ds(pl.multiple_of(b * cb, cb), cb)
            raw = lax.dot_general(
                c_ref[rows, :].astype(bf16),
                fr_ref[:size, :],
                (((1,), (1,)), ((), ())),
                preferred_element_type=f32,
            )
            m = jnp.max(raw, axis=0, keepdims=True)
            e = jnp.exp2((raw - m) * k)
            e_ref[rows, :size] = e.astype(bf16)
            mb_ref[b, :, :size] = jnp.broadcast_to(m, (8, size))
            new = jnp.maximum(top, m)
            tot = tot * jnp.exp2((top - new) * k) + jnp.sum(e, axis=0, keepdims=True) * jnp.exp2(
                (m - new) * k
            )
            return new, tot

        top, tot = lax.fori_loop(
            0, steps, step, (jnp.full((1, size), -1e30, f32), jnp.zeros((1, size), f32)), unroll=2
        )
        st_ref[0:1, :size] = top
        st_ref[1:2, :size] = tot

    for i, size in enumerate(sizes):
        over = total > (sizes[i - 1] if i else -1)
        within = total <= size if size < frames else True
        pl.when(jnp.logical_and(over, within))(functools.partial(run, size))


def refresh_body(k, cb, sizes, c_ref, fr_ref, e_ref, mb_ref, n_ref, *refs):
    stats, (o_ref, out_buf, sem) = refs[:-3], refs[-3:]
    cents, width = c_ref.shape
    frames = fr_ref.shape[0]
    steps = cents // cb
    total = n_ref[0]

    def run(size):
        top = functools.reduce(jnp.maximum, [s[0:1, :size] for s in stats])
        denom = functools.reduce(
            jnp.add, [s[1:2, :size] * jnp.exp2((s[0:1, :size] - top) * k) for s in stats]
        )
        valid = lax.broadcasted_iota(jnp.int32, (1, size), 1) < total
        keep = jnp.where(valid, 1.0 / denom, 0.0)

        def out_copy(slot, rows):
            return pltpu.make_async_copy(out_buf.at[slot], o_ref.at[rows, :], sem.at[slot])

        def step(b, _):
            rows = pl.ds(pl.multiple_of(b * cb, cb), cb)
            scale = jnp.exp2((mb_ref[b * cb // mb_rows, 0:1, :size] - top) * k) * keep
            w = (e_ref[rows, :size].astype(f32) * scale).astype(bf16)
            sums = lax.dot_general(
                w, fr_ref[:size, :], (((1,), (0,)), ((), ())), preferred_element_type=f32
            )
            soft = jnp.sum(w.astype(f32), axis=1, keepdims=True)
            slot = lax.rem(b, 2)

            @pl.when(b >= 2)
            def _():
                out_copy(slot, rows).wait()

            out_buf[slot] = (sums + prior_weight * c_ref[rows, :]) * (1.0 / (soft + prior_weight))
            out_copy(slot, rows).start()
            return 0

        mb_rows = cents // mb_ref.shape[0]
        lax.fori_loop(0, steps, step, 0)
        for slot in range(2):
            out_copy(slot, pl.ds(0, cb)).wait()

    for i, size in enumerate(sizes):
        over = total > (sizes[i - 1] if i else -1)
        within = total <= size if size < frames else True
        pl.when(jnp.logical_and(over, within))(functools.partial(run, size))


VMEM = pl.BlockSpec(memory_space=pltpu.VMEM)
SMEM = pl.BlockSpec(memory_space=pltpu.SMEM)


def exchange(x, axis, size):
    return [lax.ppermute(x, axis, [(i, i ^ d) for i in range(size)]) for d in range(1, size)]


def fast(sizes, latents, valid_mask, centroids):
    cents, width = centroids.shape
    k = 3.0 / math.sqrt(width) * math.log2(math.e)
    section, grp, cent = sizes["section"], sizes["grp"], sizes["cent"]
    blocks = section * grp * cent
    frames = -(-blocks * VMAX // LANES) * LANES
    batch = [s for s in (frames * 4 // 5 // LANES * LANES,) if s] + [frames]
    cb_a, cb_b = min(512, cents), min(256, cents)

    packed = pl.pallas_call(
        functools.partial(pack_body, (("section", section), ("grp", grp), ("cent", cent))),
        in_specs=[VMEM, VMEM],
        out_specs=VMEM,
        out_shape=jax.ShapeDtypeStruct((ROWS, width + 2 * LANES), bf16),
        name="pack",
    )(latents, valid_mask[None, :])

    column = jnp.stack([packed] + exchange(packed, "grp", grp))
    half = [column] + exchange(column, "section", section)
    parts = half + [x for h in half for x in exchange(h, "cent", cent)]

    held = pltpu.with_memory_space_constraint(centroids, pltpu.VMEM)
    steps = cents // cb_a
    frame_rows, e, mb, stats, total = pl.pallas_call(
        functools.partial(scores_body, k, cb_a, batch),
        in_specs=[VMEM] * (1 + len(parts)),
        out_specs=[VMEM] * 4 + [SMEM],
        out_shape=[
            pltpu.VMEM((frames, width), bf16),
            pltpu.VMEM((cents, frames), bf16),
            pltpu.VMEM((steps, 8, frames), f32),
            jax.ShapeDtypeStruct((8, frames), f32),
            jax.ShapeDtypeStruct((1,), jnp.int32),
        ],
        scratch_shapes=[
            pltpu.VMEM((blocks * ROWS, width), bf16),
            pltpu.VMEM((blocks * ROWS, LANES), f32),
            pltpu.VMEM((blocks * ROWS, LANES), f32),
        ],
        compiler_params=pltpu.CompilerParams(vmem_limit_bytes=12 << 20),
        name="scores",
    )(held, *parts)

    def merge(a, b):
        top = jnp.maximum(a[0:1], b[0:1])
        tot = a[1:2] * jnp.exp2((a[0:1] - top) * k) + b[1:2] * jnp.exp2((b[0:1] - top) * k)
        return jnp.concatenate([top, tot, jnp.zeros_like(a[2:])], axis=0)

    for other in exchange(stats, "cent", cent):
        stats = merge(stats, other)
    all_stats = [stats] + exchange(stats, "section", section)

    return pl.pallas_call(
        functools.partial(refresh_body, k, cb_b, batch),
        in_specs=[VMEM] * 4 + [SMEM] + [VMEM] * len(all_stats),
        out_specs=pl.BlockSpec(memory_space=pl.ANY),
        out_shape=jax.ShapeDtypeStruct((cents, width), f32),
        scratch_shapes=[pltpu.VMEM((2, cb_b, width), f32), pltpu.SemaphoreType.DMA((2,))],
        compiler_params=pltpu.CompilerParams(vmem_limit_bytes=8 << 20),
        name="refresh",
    )(held, frame_rows, e, mb, total, *all_stats)


def general(latents, valid_mask, centroids):
    width = centroids.shape[1]
    frame_rows = lax.all_gather(latents[:VMAX], ("section", "cent"), axis=0, tiled=True)
    frame_flags = lax.all_gather(valid_mask[:VMAX], ("section", "cent"), axis=0, tiled=True)
    scores = lax.dot_general(
        frame_rows,
        centroids.astype(bf16),
        (((1,), (1,)), ((), ())),
        preferred_element_type=f32,
    ) * (3.0 / math.sqrt(width))
    row_max = lax.pmax(jnp.max(scores, axis=1), ("section", "cent"))
    row_total = lax.psum(jnp.sum(jnp.exp(scores - row_max[:, None]), axis=1), ("section", "cent"))
    weights = (
        frame_flags.astype(f32)[:, None] * jnp.exp(scores - row_max[:, None]) / row_total[:, None]
    ).astype(bf16)
    sums = lax.dot_general(
        weights, frame_rows, (((0,), (0,)), ((), ())), preferred_element_type=f32
    )
    soft = jnp.sum(weights, axis=0, dtype=f32)
    sums, soft = lax.psum((sums, soft), "grp")
    return (sums + prior_weight * centroids) / (soft + prior_weight)[:, None]


def solution(mesh):
    sizes = dict(mesh.shape)
    blocks = sizes["section"] * sizes["grp"] * sizes["cent"]

    def per_device(latents, valid_mask, centroids):
        cents, width = centroids.shape
        powers = all(n & (n - 1) == 0 for n in sizes.values())
        folds = (VMAX - ROWS) * width == ROWS * LANES
        if powers and folds and blocks <= 32 and cents % 512 == 0 and cents <= 8192:
            return fast(sizes, latents, valid_mask, centroids)
        return general(latents, valid_mask, centroids)

    return jax.shard_map(
        per_device,
        mesh=mesh,
        in_specs=(
            P(("section", "grp", "cent"), None),
            P(("section", "grp", "cent")),
            P(("section", "cent"), None),
        ),
        out_specs=P(("section", "cent"), None),
        check_vma=False,
    )
```

time: 1230 us -> 104 us (0.08)
  waiting for transfers between devices: 1080 us -> 15.5 us
  blocking collectives: 65 us -> 0 us
  Pallas kernels: 0 us -> 42.2 us
  other arithmetic: 39.5 us -> 1.7 us
  matrix products: 29.9 us -> 0 us
  local copies, waits for them, and re-layouts: 2.89 us -> 30.3 us
  between operations: 14.1 us -> 0.09 us
  starting transfers between devices: 0.01 us -> 13.3 us
    psum x1 -> x0, waiting for transfers between devices: 1080 us -> none  [per_device(): total_sums, total_counts = lax.psum((center_sums, soft_counts), 'grp')]
    pallas_call x0 -> x3, Pallas kernels: none -> 42.2 us  [the longest x1 23.9 us: fast(): pl.pallas_call(functools.partial(refresh_body, k, cb_b, batch), in_specs=...]
    psum x2 -> x0, blocking collectives: 33.4 us -> none  [the longest x1 21.6 us: per_device(): total_sums, total_counts = lax.psum((center_sums, soft_counts), 'grp')]
    div x1 -> x0, other arithmetic: 32.9 us -> none  [per_device(): (total_sums + prior_weight * centroids) / (total_counts + prior_weight)[:...]
    dot_general x2 -> x0, matrix products: 29.9 us -> none  [the longest x1 15.7 us: per_device(): lax.dot_general(frame_rows, cent_low, (((1,), (1,)), ((), ())), preferred...]
    unnamed x5 -> x24, local copies, waits for them, and re-layouts: 2.89 us -> 30.2 us
    ppermute x0 -> x14, waiting for transfers between devices: none -> 15.5 us  [exchange(): lax.ppermute(x, axis, [(i, i ^ d) for i in range(size)])]
    ppermute x0 -> x14, starting transfers between devices: none -> 13.3 us  [exchange(): lax.ppermute(x, axis, [(i, i ^ d) for i in range(size)])]
  transfers between devices with their start and end apart: 1 -> 14, of which waited for: 1 -> 11; matrix products, arithmetic and copies ran while one was open for 0% -> 0% of each run, Pallas kernels for 0% -> 0%
where the time goes in v1:
time: 104 us; the launch traced here: 103 us
  Pallas kernels  42.2 us (41%)
  local copies, waits for them, and re-layouts  30.3 us (29%)
  waiting for transfers between devices  15.5 us (15%)
  starting transfers between devices  13.3 us (13%)
  other arithmetic  1.7 us (2%)
    unnamed x24, local copies, waits for them, and re-layouts  30.2 us
    pallas_call x1, Pallas kernels, fast(): pl.pallas_call(functools.partial(refresh_body, k, cb_b, batch), in_specs=...  23.9 us
    pallas_call x1, Pallas kernels, fast(): pl.pallas_call(functools.partial(scores_body, k, cb_a, batch), in_specs=[...  16.8 us
    ppermute x14, waiting for transfers between devices, exchange(): lax.ppermute(x, axis, [(i, i ^ d) for i in range(size)])  15.5 us
    ppermute x14, starting transfers between devices, exchange(): lax.ppermute(x, axis, [(i, i ^ d) for i in range(size)])  13.3 us
  transfers between devices with their start and end apart: 14, of which 11 were waited for; matrix products, arithmetic and copies ran while one was open for 0% of the time, Pallas kernels for 0%

profile of v1, /device:TPU:0, one launch (start us, length us, event | category | flops | bytes accessed | tf_op | source)
XLA Modules:
  0.0 103.1 jit_solution(8075410558271859625)
XLA Ops:
  0.0 1.5 %pack.1 = bf16[16,1280]{1,0:T(8,128)(2,1)} custom-call(bf16[24,1024]{1,0:T(8,128)(2,1)} %lat_ref.1, s32[1,24]{1,0:T(1,128)} %bitcast.9), custom_call_target="tpu_custom_call" | custom-call | tf_op jit(solution)/shard_map/pack/pallas_call | solution.py:190
  1.5 5.0 %collective-permute-start.2 = (bf16[16,1280]{1,0:T(8,128)(2,1)}, bf16[16,1280]{1,0:T(8,128)(2,1)S(1)}, u32[]{:S(2)}, u32[]{:S(2)}) collective-permute-start(bf16[16,1280]{1,0:T(8,128)(2,1)} %pack.1), channel_id=1, source_target_pairs={{0,6},{2,4},{4,2},{6,0},{1,7},{3,5},{5,3},{7,1},{8,14},{10,12},{12... | collective-permute-start | bytes 122888 | tf_op jit(solution)/shard_map/ppermute | solution.py:178
  6.6 0.6 collective-permute-start
  7.1 1.6 %collective-permute-done.2 = bf16[16,1280]{1,0:T(8,128)(2,1)S(1)} collective-permute-done((bf16[16,1280]{1,0:T(8,128)(2,1)}, bf16[16,1280]{1,0:T(8,128)(2,1)S(1)}, u32[]{:S(2)}, u32[]{:S(2)}) %collective-permute-start.2) | collective-permute-done | bytes 40992 | tf_op jit(solution)/shard_map/ppermute | solution.py:178
  8.8 2.9 %collective-permute-done.1 = bf16[16,1280]{1,0:T(8,128)(2,1)S(1)} collective-permute-done((bf16[16,1280]{1,0:T(8,128)(2,1)}, bf16[16,1280]{1,0:T(8,128)(2,1)S(1)}, u32[]{:S(2)}, u32[]{:S(2)}) %collective-permute-start.1) | collective-permute-done | bytes 40992 | tf_op jit(solution)/shard_map/ppermute | solution.py:178
  11.7 0.8 pad_maximum_fusion.refs_0_
  12.5 2.5 %collective-permute-start.5 = (bf16[4,16,1280]{2,1,0:T(8,128)(2,1)S(1)}, bf16[4,16,1280]{2,1,0:T(8,128)(2,1)S(1)}, u32[]{:S(2)}, u32[]{:S(2)}) collective-permute-start(bf16[4,16,1280]{2,1,0:T(8,128)(2,1)S(1)} %pad_maximum_fusion.refs_0_), channel_id=1, source_target_pairs={{0,24},{8,16},{16,8},{24,0},{1,25},{9,17},{17,9},{25,1},{2,26},{10... | collective-permute-start | bytes 491528 | tf_op jit(solution)/shard_map/ppermute | solution.py:178
  16.0 4.5 %collective-permute-done.5.refs_3_ = bf16[4,16,1280]{2,1,0:T(8,128)(2,1)S(1)} collective-permute-done((bf16[4,16,1280]{2,1,0:T(8,128)(2,1)S(1)}, bf16[4,16,1280]{2,1,0:T(8,128)(2,1)S(1)}, u32[]{:S(2)}, u32[]{:S(2)}) %collective-permute-start.5) | collective-permute-done | bytes 163872 | tf_op jit(solution)/shard_map/ppermute | solution.py:178
  20.5 0.9 collective-permute-done.4.refs_2_
  22.0 0.9 collective-permute-done.8.refs_6_
  23.5 0.7 copy-done.11
  24.2 10.5 %copy-done = f32[8192,1024]{1,0:T(8,128)S(1)} copy-done((f32[8192,1024]{1,0:T(8,128)S(1)}, f32[8192,1024]{1,0:T(8,128)}, u32[]{:S(2)}) %copy-start) | copy-done | bytes 33554456
  34.7 16.8 %scores.1 = (bf16[640,1024]{1,0:T(8,128)(2,1)S(1)}, bf16[8192,640]{1,0:T(8,128)(2,1)S(1)}, f32[16,8,640]{2,1,0:T(8,128)S(1)}, f32[8,640]{1,0:T(8,128)}, s32[1]{0:T(128)}) custom-call(f32[8192,1024]{1,0:T(8,128)S(1)} %copy-done, bf16[4,16,1280]{2,1,0:T(8,128)(2,1)} %copy-done.4, bf16[4,16,1280]{2,1,0:T(8,128)(2,1)} %copy-done.7, ...), custom_call_target="tpu_custom_call" | custom-call | tf_op jit(solution)/shard_map/scores/pallas_call | solution.py:204
  51.6 4.1 %copy-done.2 = bf16[8192,640]{1,0:T(8,128)(2,1)} copy-done((bf16[8192,640]{1,0:T(8,128)(2,1)}, bf16[8192,640]{1,0:T(8,128)(2,1)S(1)}, u32[]{:S(2)}) %copy-start.2) | copy-done | bytes 10485784
  55.9 1.2 %collective-permute-done.10 = f32[8,640]{1,0:T(8,128)S(1)} collective-permute-done((f32[8,640]{1,0:T(8,128)}, f32[8,640]{1,0:T(8,128)S(1)}, u32[]{:S(2)}, u32[]{:S(2)}) %collective-permute-start.10) | collective-permute-done | bytes 20512 | tf_op jit(solution)/shard_map/ppermute | solution.py:178
  57.1 0.8 fusion
  58.0 1.8 %collective-permute-start.13 = (f32[8,640]{1,0:T(8,128)S(1)}, f32[8,640]{1,0:T(8,128)S(1)}, u32[]{:S(2)}, u32[]{:S(2)}) collective-permute-start(f32[8,640]{1,0:T(8,128)S(1)} %maximum_maximum_fusion.refs_0_), channel_id=1, source_target_pairs={{0,24},{8,16},{16,8},{24,0},{1,25},{9,17},{17,9},{25,1},{2,26},{10... | collective-permute-start | bytes 61448 | tf_op jit(solution)/shard_map/ppermute | solution.py:178
  59.7 1.2 %collective-permute-start.12 = (f32[8,640]{1,0:T(8,128)S(1)}, f32[8,640]{1,0:T(8,128)S(1)}, u32[]{:S(2)}, u32[]{:S(2)}) collective-permute-start(f32[8,640]{1,0:T(8,128)S(1)} %maximum_maximum_fusion.refs_0_), channel_id=1, source_target_pairs={{0,16},{8,24},{16,0},{24,8},{1,17},{9,25},{17,1},{25,9},{2,18},{10... | collective-permute-start | bytes 61448 | tf_op jit(solution)/shard_map/ppermute | solution.py:178
  61.5 1.2 %collective-permute-done.13.refs_3_ = f32[8,640]{1,0:T(8,128)S(1)} collective-permute-done((f32[8,640]{1,0:T(8,128)S(1)}, f32[8,640]{1,0:T(8,128)S(1)}, u32[]{:S(2)}, u32[]{:S(2)}) %collective-permute-start.13) | collective-permute-done | bytes 20512 | tf_op jit(solution)/shard_map/ppermute | solution.py:178
  62.7 0.8 collective-permute-done.12.refs_2_
  63.5 1.2 %collective-permute-done.11.refs_1_ = f32[8,640]{1,0:T(8,128)S(1)} collective-permute-done((f32[8,640]{1,0:T(8,128)S(1)}, f32[8,640]{1,0:T(8,128)S(1)}, u32[]{:S(2)}, u32[]{:S(2)}) %collective-permute-start.11) | collective-permute-done | bytes 20512 | tf_op jit(solution)/shard_map/ppermute | solution.py:178
  64.7 10.5 %copy-done.1 = f32[8192,1024]{1,0:T(8,128)S(1)} copy-done((f32[8192,1024]{1,0:T(8,128)S(1)}, f32[8192,1024]{1,0:T(8,128)}, u32[]{:S(2)}) %copy-start.1) | copy-done | bytes 33554456
  75.3 4.0 %copy-done.3 = bf16[8192,640]{1,0:T(8,128)(2,1)S(1)} copy-done((bf16[8192,640]{1,0:T(8,128)(2,1)S(1)}, bf16[8192,640]{1,0:T(8,128)(2,1)}, u32[]{:S(2)}) %copy-start.3) | copy-done | bytes 10485784
  79.2 23.9 %refresh.1 = f32[8192,1024]{1,0:T(8,128)} custom-call(f32[8192,1024]{1,0:T(8,128)S(1)} %copy-done.1, bf16[640,1024]{1,0:T(8,128)(2,1)S(1)} %get-tuple-element.10.fr_ref, bf16[8192,640]{1,0:T(8,128)(2,1)S(1)} %copy-done.3, f32[16,8,640]{2,1,0:T(8,128)S(1)} %get-tuple-element.12.mb_ref, s32[1]{0:T(128)} %get-tuple-element.13.n_ref, ...), custom_call_target="tpu_custom_call" | custom-call | tf_op jit(solution)/shard_map/refresh/pallas_call | solution.py:233
  (36 shorter events, 3.1 us)
Async XLA Ops:
  1.5 7.3 %collective-permute-start.2 = (bf16[16,1280]{1,0:T(8,128)(2,1)}, bf16[16,1280]{1,0:T(8,128)(2,1)S(1)}, u32[]{:S(2)}, u32[]{:S(2)}) collective-permute-start(bf16[16,1280]{1,0:T(8,128)(2,1)} %pack.1), channel_id=1, source_target_pairs={{0,6},{2,4},{4,2},{6,0},{1,7},{3,5},{5,3},{7,1},{8,14},{10,12},{12... | collective-permute-start | bytes 122888 | tf_op jit(solution)/shard_map/ppermute | solution.py:178
  6.5 5.1 %collective-permute-start.1 = (bf16[16,1280]{1,0:T(8,128)(2,1)}, bf16[16,1280]{1,0:T(8,128)(2,1)S(1)}, u32[]{:S(2)}, u32[]{:S(2)}) collective-permute-start(bf16[16,1280]{1,0:T(8,128)(2,1)} %pack.1), channel_id=1, source_target_pairs={{0,4},{2,6},{4,0},{6,2},{1,5},{3,7},{5,1},{7,3},{8,12},{10,14},{12... | collective-permute-start | bytes 122888 | tf_op jit(solution)/shard_map/ppermute | solution.py:178
  6.6 5.1 %collective-permute-start = (bf16[16,1280]{1,0:T(8,128)(2,1)}, bf16[16,1280]{1,0:T(8,128)(2,1)S(1)}, u32[]{:S(2)}, u32[]{:S(2)}) collective-permute-start(bf16[16,1280]{1,0:T(8,128)(2,1)} %pack.1), channel_id=1, source_target_pairs={{0,2},{2,0},{4,6},{6,4},{1,3},{3,1},{5,7},{7,5},{8,10},{10,8},{12,... | collective-permute-start | bytes 122888 | tf_op jit(solution)/shard_map/ppermute | solution.py:178
  12.5 10.6 %copy-start.4 = (bf16[4,16,1280]{2,1,0:T(8,128)(2,1)}, bf16[4,16,1280]{2,1,0:T(8,128)(2,1)S(1)}, u32[]{:S(2)}) copy-start(bf16[4,16,1280]{2,1,0:T(8,128)(2,1)S(1)} %pad_maximum_fusion.refs_0_) | copy-start | bytes 491524
  12.5 8.0 %collective-permute-start.5 = (bf16[4,16,1280]{2,1,0:T(8,128)(2,1)S(1)}, bf16[4,16,1280]{2,1,0:T(8,128)(2,1)S(1)}, u32[]{:S(2)}, u32[]{:S(2)}) collective-permute-start(bf16[4,16,1280]{2,1,0:T(8,128)(2,1)S(1)} %pad_maximum_fusion.refs_0_), channel_id=1, source_target_pairs={{0,24},{8,16},{16,8},{24,0},{1,25},{9,17},{17,9},{25,1},{2,26},{10... | collective-permute-start | bytes 491528 | tf_op jit(solution)/shard_map/ppermute | solution.py:178
  15.0 6.5 %collective-permute-start.4 = (bf16[4,16,1280]{2,1,0:T(8,128)(2,1)S(1)}, bf16[4,16,1280]{2,1,0:T(8,128)(2,1)S(1)}, u32[]{:S(2)}, u32[]{:S(2)}) collective-permute-start(bf16[4,16,1280]{2,1,0:T(8,128)(2,1)S(1)} %pad_maximum_fusion.refs_0_), channel_id=1, source_target_pairs={{0,16},{8,24},{16,0},{24,8},{1,17},{9,25},{17,1},{25,9},{2,18},{10... | collective-permute-start | bytes 491528 | tf_op jit(solution)/shard_map/ppermute | solution.py:178
  15.5 6.0 %collective-permute-start.3 = (bf16[4,16,1280]{2,1,0:T(8,128)(2,1)S(1)}, bf16[4,16,1280]{2,1,0:T(8,128)(2,1)S(1)}, u32[]{:S(2)}, u32[]{:S(2)}) collective-permute-start(bf16[4,16,1280]{2,1,0:T(8,128)(2,1)S(1)} %pad_maximum_fusion.refs_0_), channel_id=1, source_target_pairs={{0,8},{8,0},{16,24},{24,16},{1,9},{9,1},{17,25},{25,17},{2,10},{10... | collective-permute-start | bytes 491528 | tf_op jit(solution)/shard_map/ppermute | solution.py:178
  16.0 6.0 %collective-permute-start.6 = (bf16[4,16,1280]{2,1,0:T(8,128)(2,1)S(1)}, bf16[4,16,1280]{2,1,0:T(8,128)(2,1)S(1)}, u32[]{:S(2)}, u32[]{:S(2)}) collective-permute-start(bf16[4,16,1280]{2,1,0:T(8,128)(2,1)S(1)} %pad_maximum_fusion.refs_0_), channel_id=1, source_target_pairs={{0,1},{1,0},{2,3},{3,2},{4,5},{5,4},{6,7},{7,6},{8,9},{9,8},{10,11... | collective-permute-start | bytes 491528 | tf_op jit(solution)/shard_map/ppermute | solution.py:178
  20.5 2.6 %copy-start.5 = (bf16[4,16,1280]{2,1,0:T(8,128)(2,1)}, bf16[4,16,1280]{2,1,0:T(8,128)(2,1)S(1)}, u32[]{:S(2)}) copy-start(bf16[4,16,1280]{2,1,0:T(8,128)(2,1)S(1)} %collective-permute-done.5.refs_3_) | copy-start | bytes 491524
  20.5 1.5 %collective-permute-start.9 = (bf16[4,16,1280]{2,1,0:T(8,128)(2,1)S(1)}, bf16[4,16,1280]{2,1,0:T(8,128)(2,1)S(1)}, u32[]{:S(2)}, u32[]{:S(2)}) collective-permute-start(bf16[4,16,1280]{2,1,0:T(8,128)(2,1)S(1)} %collective-permute-done.5.refs_3_), channel_id=1, source_target_pairs={{0,1},{1,0},{2,3},{3,2},{4,5},{5,4},{6,7},{7,6},{8,9},{9,8},{10,11... | collective-permute-start | bytes 491528 | tf_op jit(solution)/shard_map/ppermute | solution.py:178
  21.5 1.6 %copy-start.6 = (bf16[4,16,1280]{2,1,0:T(8,128)(2,1)}, bf16[4,16,1280]{2,1,0:T(8,128)(2,1)S(1)}, u32[]{:S(2)}) copy-start(bf16[4,16,1280]{2,1,0:T(8,128)(2,1)S(1)} %collective-permute-done.4.refs_2_) | copy-start | bytes 491524
  21.5 1.4 %collective-permute-start.8 = (bf16[4,16,1280]{2,1,0:T(8,128)(2,1)S(1)}, bf16[4,16,1280]{2,1,0:T(8,128)(2,1)S(1)}, u32[]{:S(2)}, u32[]{:S(2)}) collective-permute-start(bf16[4,16,1280]{2,1,0:T(8,128)(2,1)S(1)} %collective-permute-done.4.refs_2_), channel_id=1, source_target_pairs={{0,1},{1,0},{2,3},{3,2},{4,5},{5,4},{6,7},{7,6},{8,9},{9,8},{10,11... | collective-permute-start | bytes 491528 | tf_op jit(solution)/shard_map/ppermute | solution.py:178
  21.5 1.6 %copy-start.7 = (bf16[4,16,1280]{2,1,0:T(8,128)(2,1)}, bf16[4,16,1280]{2,1,0:T(8,128)(2,1)S(1)}, u32[]{:S(2)}) copy-start(bf16[4,16,1280]{2,1,0:T(8,128)(2,1)S(1)} %collective-permute-done.3.refs_1_) | copy-start | bytes 491524
  21.5 1.6 %collective-permute-start.7 = (bf16[4,16,1280]{2,1,0:T(8,128)(2,1)S(1)}, bf16[4,16,1280]{2,1,0:T(8,128)(2,1)S(1)}, u32[]{:S(2)}, u32[]{:S(2)}) collective-permute-start(bf16[4,16,1280]{2,1,0:T(8,128)(2,1)S(1)} %collective-permute-done.3.refs_1_), channel_id=1, source_target_pairs={{0,1},{1,0},{2,3},{3,2},{4,5},{5,4},{6,7},{7,6},{8,9},{9,8},{10,11... | collective-permute-start | bytes 491528 | tf_op jit(solution)/shard_map/ppermute | solution.py:178
  22.0 1.1 %copy-start.8 = (bf16[4,16,1280]{2,1,0:T(8,128)(2,1)}, bf16[4,16,1280]{2,1,0:T(8,128)(2,1)S(1)}, u32[]{:S(2)}) copy-start(bf16[4,16,1280]{2,1,0:T(8,128)(2,1)S(1)} %collective-permute-done.6.refs_4_) | copy-start | bytes 491524
  22.0 1.1 %copy-start.9 = (bf16[4,16,1280]{2,1,0:T(8,128)(2,1)}, bf16[4,16,1280]{2,1,0:T(8,128)(2,1)S(1)}, u32[]{:S(2)}) copy-start(bf16[4,16,1280]{2,1,0:T(8,128)(2,1)S(1)} %collective-permute-done.9.refs_7_) | copy-start | bytes 491524
  24.2 10.5 %copy-start = (f32[8192,1024]{1,0:T(8,128)S(1)}, f32[8192,1024]{1,0:T(8,128)}, u32[]{:S(2)}) copy-start(f32[8192,1024]{1,0:T(8,128)} %c_ref.3) | copy-start | bytes 100663296
  51.6 4.1 %copy-start.2 = (bf16[8192,640]{1,0:T(8,128)(2,1)}, bf16[8192,640]{1,0:T(8,128)(2,1)S(1)}, u32[]{:S(2)}) copy-start(bf16[8192,640]{1,0:T(8,128)(2,1)S(1)} %get-tuple-element.11.e_ref) | copy-start | bytes 31457284
  55.7 1.4 %collective-permute-start.10 = (f32[8,640]{1,0:T(8,128)}, f32[8,640]{1,0:T(8,128)S(1)}, u32[]{:S(2)}, u32[]{:S(2)}) collective-permute-start(f32[8,640]{1,0:T(8,128)} %get-tuple-element.14), channel_id=1, source_target_pairs={{0,1},{1,0},{2,3},{3,2},{4,5},{5,4},{6,7},{7,6},{8,9},{9,8},{10,11... | collective-permute-start | bytes 61448 | tf_op jit(solution)/shard_map/ppermute | solution.py:178
  58.0 4.7 %collective-permute-start.13 = (f32[8,640]{1,0:T(8,128)S(1)}, f32[8,640]{1,0:T(8,128)S(1)}, u32[]{:S(2)}, u32[]{:S(2)}) collective-permute-start(f32[8,640]{1,0:T(8,128)S(1)} %maximum_maximum_fusion.refs_0_), channel_id=1, source_target_pairs={{0,24},{8,16},{16,8},{24,0},{1,25},{9,17},{17,9},{25,1},{2,26},{10... | collective-permute-start | bytes 61448 | tf_op jit(solution)/shard_map/ppermute | solution.py:178
  59.7 3.8 %collective-permute-start.12 = (f32[8,640]{1,0:T(8,128)S(1)}, f32[8,640]{1,0:T(8,128)S(1)}, u32[]{:S(2)}, u32[]{:S(2)}) collective-permute-start(f32[8,640]{1,0:T(8,128)S(1)} %maximum_maximum_fusion.refs_0_), channel_id=1, source_target_pairs={{0,16},{8,24},{16,0},{24,8},{1,17},{9,25},{17,1},{25,9},{2,18},{10... | collective-permute-start | bytes 61448 | tf_op jit(solution)/shard_map/ppermute | solution.py:178
  60.9 3.8 %collective-permute-start.11 = (f32[8,640]{1,0:T(8,128)S(1)}, f32[8,640]{1,0:T(8,128)S(1)}, u32[]{:S(2)}, u32[]{:S(2)}) collective-permute-start(f32[8,640]{1,0:T(8,128)S(1)} %maximum_maximum_fusion.refs_0_), channel_id=1, source_target_pairs={{0,8},{8,0},{16,24},{24,16},{1,9},{9,1},{17,25},{25,17},{2,10},{10... | collective-permute-start | bytes 61448 | tf_op jit(solution)/shard_map/ppermute | solution.py:178
  64.7 10.5 %copy-start.1 = (f32[8192,1024]{1,0:T(8,128)S(1)}, f32[8192,1024]{1,0:T(8,128)}, u32[]{:S(2)}) copy-start(f32[8192,1024]{1,0:T(8,128)} %c_ref.3) | copy-start | bytes 100663296
  75.3 4.0 %copy-start.3 = (bf16[8192,640]{1,0:T(8,128)(2,1)S(1)}, bf16[8192,640]{1,0:T(8,128)(2,1)}, u32[]{:S(2)}) copy-start(bf16[8192,640]{1,0:T(8,128)(2,1)} %copy-done.2) | copy-start | bytes 31457284
  (2 other events, 1.3 us)

commit v2 on v1

v2 whole, which is shorter than its diff:
```python
import functools
import math

import jax
import jax.numpy as jnp
from jax import lax
from jax.experimental import pallas as pl
from jax.experimental.pallas import tpu as pltpu
from jax.sharding import PartitionSpec as P

VMAX = 18
LANES = 128
SCOPE = 9 << 20
ROWS = 16
f32, bf16 = jnp.float32, jnp.bfloat16

prior_weight = 0.05


def pack_body(axes, lat_ref, mask_ref, out_ref):
    width = lat_ref.shape[1]
    rows = lat_ref[...].astype(f32)
    fold = width // LANES
    pieces = [
        rows[r : r + 1, j * LANES : (j + 1) * LANES] for r in range(ROWS, VMAX) for j in range(fold)
    ]
    count = jnp.sum(mask_ref[...].astype(f32), axis=1, keepdims=True)
    block = jnp.int32(0)
    for name, size in axes:
        block = block * size + lax.axis_index(name)
    lane = lax.broadcasted_iota(jnp.int32, (ROWS, LANES), 1)
    tail = jnp.where(lane == 0, count, jnp.where(lane == 1, block.astype(f32), 0.0))
    out_ref[:, :width] = rows[:ROWS].astype(bf16)
    out_ref[:, width : width + LANES] = jnp.concatenate(pieces, axis=0).astype(bf16)
    out_ref[:, width + LANES :] = tail.astype(bf16)


def by_size(total, plans, run):
    for i, (size, *plan) in enumerate(plans):
        over = total > (plans[i - 1][0] if i else -1)
        within = total <= size if i + 1 < len(plans) else True
        pl.when(jnp.logical_and(over, within))(functools.partial(run, size, *plan))


def stack_body(*refs):
    for i, ref in enumerate(refs[:-1]):
        refs[-1][i] = ref[...]


def load_body(pieces, which, _, c_hbm, *refs):
    *c_refs, sem = refs[-pieces - 1 :]
    piece = c_refs[0].shape[0]
    copies = [
        pltpu.make_async_copy(c_hbm.at[pl.ds(i * piece, piece), :], c_refs[i], sem.at[i])
        for i in which
    ]
    for copy in copies:
        copy.start()
    for copy in copies:
        copy.wait()


def order_body(parts, *refs):
    packed, (fr_ref, n_ref, all_ref, ext_ref, meta_ref) = refs[:parts], refs[parts:]
    frames, width = fr_ref.shape

    at = 0
    for part in packed:
        for i in range(part.shape[0]):
            all_ref[at : at + ROWS, :] = part[i, :, :width]
            ext_ref[at : at + ROWS, :] = part[i, :, width : width + LANES].astype(f32)
            meta_ref[at : at + ROWS, :] = part[i, :, width + LANES :].astype(f32)
            at += ROWS
    blocks = at // ROWS
    meta = meta_ref[pl.ds(0, blocks, stride=ROWS), :]
    count, number = meta[:, 0:1], meta[:, 1:2]
    total = jnp.sum(count)
    n_ref[0] = total.astype(jnp.int32)

    def place(rows, block_of, row_of):
        block = lax.broadcasted_iota(jnp.int32, (blocks, rows), 0)
        r = lax.broadcasted_iota(jnp.int32, (blocks, rows), 1)
        mine = block == block_of(r)
        length = jnp.sum(jnp.where(mine, count, 0.0), axis=0, keepdims=True)
        own = jnp.sum(jnp.where(mine, number, 0.0), axis=0, keepdims=True)
        before = jnp.sum(jnp.where(number < own, count, 0.0), axis=0, keepdims=True)
        row = row_of(lax.broadcasted_iota(jnp.int32, (1, rows), 1)).astype(f32)
        return jnp.where(row < length, before + row, -1.0)

    def one_hot(to, start, rows):
        p = lax.broadcasted_iota(jnp.int32, (rows, to.shape[1]), 0) + start
        return jnp.where(p.astype(f32) == to, 1.0, 0.0).astype(bf16)

    extra = VMAX - ROWS
    fold = width // LANES
    main_to = place(at, lambda r: r // ROWS, lambda r: r % ROWS)
    extra_to = place(extra * blocks, lambda r: r % blocks, lambda r: ROWS + r // blocks)
    extra_rows = jnp.concatenate(
        [
            jnp.concatenate(
                [ext_ref[pl.ds(r * fold + j, blocks, stride=ROWS), :] for j in range(fold)], axis=1
            )
            for r in range(extra)
        ],
        axis=0,
    ).astype(bf16)
    chunk = LANES
    for p in range(0, frames, chunk):
        main, ext = one_hot(main_to, p, chunk), one_hot(extra_to, p, chunk)
        ordered = jnp.dot(main, all_ref[...], preferred_element_type=f32)
        ordered += jnp.dot(ext, extra_rows, preferred_element_type=f32)
        fr_ref[p : p + chunk, :] = ordered.astype(bf16)


def scores_body(k, plans, pieces, *refs):
    c_refs, refs = refs[:pieces], refs[pieces:]
    (fr_ref, n_ref), refs = refs[:2], refs[2:]
    e_refs, (mb_ref, st_ref) = refs[:pieces], refs[pieces:]
    piece = c_refs[0].shape[0]
    unit = piece * pieces // mb_ref.shape[0]

    def run(size, cb):
        def block(i, b, carry):
            top, tot = carry
            rows = pl.ds(pl.multiple_of(b * cb, cb), cb)
            raw = lax.dot_general(
                c_refs[i][rows, :].astype(bf16),
                fr_ref[:size, :],
                (((1,), (1,)), ((), ())),
                preferred_element_type=f32,
            )
            m = jnp.max(raw, axis=0, keepdims=True)
            e = jnp.exp2((raw - m) * k)
            e_refs[i][rows, :size] = e.astype(bf16)
            for j in range(cb // unit):
                at = (i * piece + b * cb) // unit + j
                mb_ref[at, :, :size] = jnp.broadcast_to(m, (8, size))
            new = jnp.maximum(top, m)
            part = jnp.sum(e, axis=0, keepdims=True)
            tot = tot * jnp.exp2((top - new) * k) + part * jnp.exp2((m - new) * k)
            return new, tot

        carry = jnp.full((1, size), -1e30, f32), jnp.zeros((1, size), f32)
        for i in range(pieces):
            carry = lax.fori_loop(0, piece // cb, functools.partial(block, i), carry)
        st_ref[...] = jnp.zeros_like(st_ref)
        st_ref[0:1, :size] = carry[0]
        st_ref[1:2, :size] = carry[1]

    by_size(n_ref[0], plans, run)


def refresh_body(k, plans, pieces, *refs):
    c_refs, refs = refs[:pieces], refs[pieces:]
    e_refs, refs = refs[:pieces], refs[pieces:]
    (fr_ref, mb_ref, n_ref), refs = refs[:3], refs[3:]
    stats, refs = refs[: -pieces - 2], refs[-pieces - 2 :]
    d_refs, (o_ref, sem) = refs[:pieces], refs[pieces:]
    piece, width = c_refs[0].shape
    total = n_ref[0]

    def run(size, cb, unroll):
        per = mb_ref.shape[0] * cb // (piece * pieces)
        top = functools.reduce(jnp.maximum, [s[0:1, :size] for s in stats])
        denom = functools.reduce(
            jnp.add, [s[1:2, :size] * jnp.exp2((s[0:1, :size] - top) * k) for s in stats]
        )
        valid = lax.broadcasted_iota(jnp.int32, (1, size), 1) < total
        keep = jnp.where(valid, 1.0 / denom, 0.0)

        def put(i, rows, to):
            return pltpu.make_async_copy(d_refs[i].at[rows, :], o_ref.at[to, :], sem.at[i])

        def block(i, b, _):
            rows = pl.ds(pl.multiple_of(b * cb, cb), cb)
            to = pl.ds(pl.multiple_of(i * piece + b * cb, cb), cb)
            scale = jnp.exp2((mb_ref[(i * (piece // cb) + b) * per, 0:1, :size] - top) * k) * keep
            w = (e_refs[i][rows, :size].astype(f32) * scale).astype(bf16)
            soft = jnp.sum(w.astype(f32), axis=1, keepdims=True)
            sums = jnp.dot(w, fr_ref[:size, :], preferred_element_type=f32)
            d_refs[i][rows, :] = (sums + prior_weight * c_refs[i][rows, :]) * (
                1.0 / (soft + prior_weight)
            )
            put(i, rows, to).start()
            return 0

        for i in range(pieces):
            lax.fori_loop(0, piece // cb, functools.partial(block, i), 0, unroll=unroll)
        for i in range(pieces):
            put(i, pl.ds(0, piece), pl.ds(i * piece, piece)).wait()

    by_size(total, plans, run)


VMEM = pl.BlockSpec(memory_space=pltpu.VMEM)
SMEM = pl.BlockSpec(memory_space=pltpu.SMEM)
HBM = pl.BlockSpec(memory_space=pltpu.HBM)


def exchange(x, axis, size):
    return [lax.ppermute(x, axis, [(i, i ^ d) for i in range(size)]) for d in range(1, size)]


def fast(sizes, latents, valid_mask, centroids):
    cents, width = centroids.shape
    k = 3.0 / math.sqrt(width) * math.log2(math.e)
    section, grp, cent = sizes["section"], sizes["grp"], sizes["cent"]
    blocks = section * grp * cent
    frames = -(-blocks * VMAX // LANES) * LANES
    small = frames * 4 // 5 // LANES * LANES
    cb = 512
    pieces = 4
    piece = cents // pieces

    packed = pl.pallas_call(
        functools.partial(pack_body, (("section", section), ("grp", grp), ("cent", cent))),
        in_specs=[VMEM, VMEM],
        out_specs=VMEM,
        out_shape=jax.ShapeDtypeStruct((ROWS, width + 2 * LANES), bf16),
        compiler_params=pltpu.CompilerParams(vmem_limit_bytes=SCOPE),
        name="pack",
    )(latents, valid_mask[None, :])

    def load(which, after, *held):
        return pl.pallas_call(
            functools.partial(load_body, pieces, which),
            in_specs=[HBM, HBM] + [VMEM] * len(held),
            out_specs=[VMEM] * pieces,
            out_shape=[pltpu.VMEM((piece, width), f32)] * pieces,
            input_output_aliases={2 + i: i for i in range(len(held))},
            scratch_shapes=[pltpu.SemaphoreType.DMA((pieces,))],
            compiler_params=pltpu.CompilerParams(vmem_limit_bytes=SCOPE),
            cost_estimate=pl.CostEstimate(
                flops=0, transcendentals=0, bytes_accessed=cents * width * 4
            ),
            name="load",
        )(after, pltpu.with_memory_space_constraint(centroids, pltpu.HBM), *held)

    others = exchange(packed, "grp", grp)
    column = pl.pallas_call(
        stack_body,
        in_specs=[VMEM] * grp,
        out_specs=VMEM,
        out_shape=jax.ShapeDtypeStruct((grp, *packed.shape), bf16),
        compiler_params=pltpu.CompilerParams(vmem_limit_bytes=SCOPE),
        name="stack",
    )(packed, *others)
    held = load(range(pieces), column)
    others, held = lax.optimization_barrier((exchange(column, "section", section), held))
    half = [column] + others
    parts = half + [x for h in half for x in exchange(h, "cent", cent)]

    frame_rows, total = pl.pallas_call(
        functools.partial(order_body, len(parts)),
        in_specs=[VMEM] * len(parts),
        out_specs=[VMEM, SMEM],
        out_shape=[
            pltpu.VMEM((frames, width), bf16),
            jax.ShapeDtypeStruct((1,), jnp.int32),
        ],
        scratch_shapes=[
            pltpu.VMEM((blocks * ROWS, width), bf16),
            pltpu.VMEM((blocks * ROWS, LANES), f32),
            pltpu.VMEM((blocks * ROWS, LANES), f32),
        ],
        compiler_params=pltpu.CompilerParams(vmem_limit_bytes=SCOPE),
        name="order",
    )(*parts)

    *e, mb, stats = pl.pallas_call(
        functools.partial(scores_body, k, ((small, cb), (frames, cb // 2)), pieces),
        in_specs=[VMEM] * (pieces + 1) + [SMEM],
        out_specs=[VMEM] * (pieces + 2),
        out_shape=[pltpu.VMEM((piece, frames), bf16)] * pieces
        + [
            pltpu.VMEM((2 * cents // cb, 8, frames), f32),
            jax.ShapeDtypeStruct((8, frames), f32),
        ],
        compiler_params=pltpu.CompilerParams(vmem_limit_bytes=SCOPE),
        name="scores",
    )(*held, frame_rows, total)

    def merge(a, b):
        top = jnp.maximum(a[0:1], b[0:1])
        tot = a[1:2] * jnp.exp2((a[0:1] - top) * k) + b[1:2] * jnp.exp2((b[0:1] - top) * k)
        return jnp.concatenate([top, tot, jnp.zeros_like(a[2:])], axis=0)

    for other in exchange(stats, "cent", cent):
        stats = merge(stats, other)
    all_stats = [stats] + exchange(stats, "section", section)

    return pl.pallas_call(
        functools.partial(refresh_body, k, ((small, cb, 2), (frames, cb // 2, 1)), pieces),
        in_specs=[VMEM] * (2 * pieces + 2) + [SMEM] + [VMEM] * len(all_stats),
        out_specs=[VMEM] * pieces + [HBM],
        out_shape=[pltpu.VMEM((piece, width), f32)] * pieces
        + [jax.ShapeDtypeStruct((cents, width), f32)],
        input_output_aliases={i: i for i in range(pieces)},
        scratch_shapes=[pltpu.SemaphoreType.DMA((pieces,))],
        compiler_params=pltpu.CompilerParams(vmem_limit_bytes=SCOPE),
        name="refresh",
    )(*held, *e, frame_rows, mb, total, *all_stats)[-1]


def general(latents, valid_mask, centroids):
    width = centroids.shape[1]
    frame_rows = lax.all_gather(latents[:VMAX], ("section", "cent"), axis=0, tiled=True)
    frame_flags = lax.all_gather(valid_mask[:VMAX], ("section", "cent"), axis=0, tiled=True)
    scores = lax.dot_general(
        frame_rows,
        centroids.astype(bf16),
        (((1,), (1,)), ((), ())),
        preferred_element_type=f32,
    ) * (3.0 / math.sqrt(width))
    row_max = lax.pmax(jnp.max(scores, axis=1), ("section", "cent"))
    row_total = lax.psum(jnp.sum(jnp.exp(scores - row_max[:, None]), axis=1), ("section", "cent"))
    weights = (
        frame_flags.astype(f32)[:, None] * jnp.exp(scores - row_max[:, None]) / row_total[:, None]
    ).astype(bf16)
    sums = lax.dot_general(
        weights, frame_rows, (((0,), (0,)), ((), ())), preferred_element_type=f32
    )
    soft = jnp.sum(weights, axis=0, dtype=f32)
    sums, soft = lax.psum((sums, soft), "grp")
    return (sums + prior_weight * centroids) / (soft + prior_weight)[:, None]


def solution(mesh):
    sizes = dict(mesh.shape)
    blocks = sizes["section"] * sizes["grp"] * sizes["cent"]

    def per_device(latents, valid_mask, centroids):
        cents, width = centroids.shape
        powers = all(n & (n - 1) == 0 for n in sizes.values())
        folds = (VMAX - ROWS) * width == ROWS * LANES
        if powers and folds and blocks <= 32 and cents % 4096 == 0 and cents <= 8192 and width <= 1024:
            return fast(sizes, latents, valid_mask, centroids)
        return general(latents, valid_mask, centroids)

    return jax.shard_map(
        per_device,
        mesh=mesh,
        in_specs=(
            P(("section", "grp", "cent"), None),
            P(("section", "grp", "cent")),
            P(("section", "cent"), None),
        ),
        out_specs=P(("section", "cent"), None),
        check_vma=False,
    )
```

time: 104 us -> 69.9 us (0.67)
  local copies, waits for them, and re-layouts: 30.3 us -> 1.53 us
  waiting for transfers between devices: 15.5 us -> 9.46 us
  Pallas kernels: 42.2 us -> 44.2 us
  other arithmetic: 1.7 us -> 0.09 us
    unnamed x24 -> x4, local copies, waits for them, and re-layouts: 30.2 us -> 1.45 us
    ppermute x14, waiting for transfers between devices: 15.5 us -> 9.46 us  [exchange(): lax.ppermute(x, axis, [(i, i ^ d) for i in range(size)])]
    pallas_call x2 -> x5, Pallas kernels: 40.7 us -> 44.1 us  [the longest x1 16.1 us: fast(): pl.pallas_call(functools.partial(scores_body, k, ((small, cb), (frames, c...]
    pallas_call x1, Pallas kernels: 1.5 us -> 0.08 us  [fast(): pl.pallas_call(functools.partial(pack_body, (('section', section), ('grp'...]
  transfers between devices with their start and end apart: 14 -> 14, of which waited for: 11 -> 9; matrix products, arithmetic and copies ran while one was open for 0% -> 0% of each run, Pallas kernels for 0% -> 15%
where the time goes in v2:
time: 69.9 us; the launch traced here: 69.7 us
  Pallas kernels  44.2 us (63%)
  starting transfers between devices  14.2 us (20%)
  waiting for transfers between devices  9.46 us (14%)
  local copies, waits for them, and re-layouts  1.53 us (2%)
    pallas_call x1, Pallas kernels, fast(): pl.pallas_call(functools.partial(scores_body, k, ((small, cb), (frames, c...  16.1 us
    pallas_call x1, Pallas kernels, fast(): pl.pallas_call(functools.partial(refresh_body, k, ((small, cb, 2), (frame...  15.7 us
    ppermute x14, starting transfers between devices, exchange(): lax.ppermute(x, axis, [(i, i ^ d) for i in range(size)])  14.2 us
    pallas_call x1, Pallas kernels, load(): pl.pallas_call(functools.partial(load_body, pieces, which), in_specs=[HBM...  10.6 us
    ppermute x14, waiting for transfers between devices, exchange(): lax.ppermute(x, axis, [(i, i ^ d) for i in range(size)])  9.46 us
    pallas_call x1, Pallas kernels, fast(): pl.pallas_call(functools.partial(order_body, len(parts)), in_specs=[VMEM]...  1.76 us
    unnamed x4, local copies, waits for them, and re-layouts  1.45 us
  transfers between devices with their start and end apart: 14, of which 9 were waited for; matrix products, arithmetic and copies ran while one was open for 0% of the time, Pallas kernels for 15%

profile of v2, /device:TPU:0, one launch (start us, length us, event | category | flops | bytes accessed | tf_op | source)
XLA Modules:
  0.0 69.7 jit_solution(11110634828103670724)
XLA Ops:
  0.0 0.8 %copy-done = bf16[24,1024]{1,0:T(8,128)(2,1)S(1)} copy-done((bf16[24,1024]{1,0:T(8,128)(2,1)S(1)}, bf16[24,1024]{1,0:T(8,128)(2,1)}, u32[]{:S(2)}) %copy-start) | copy-done | bytes 49176
  0.8 0.7 copy-done.1
  1.5 5.1 %collective-permute-start.2 = (bf16[16,1280]{1,0:T(8,128)(2,1)S(1)}, bf16[16,1280]{1,0:T(8,128)(2,1)S(1)}, u32[]{:S(2)}, u32[]{:S(2)}) collective-permute-start(bf16[16,1280]{1,0:T(8,128)(2,1)S(1)} %pack.1.refs_0_), channel_id=1, source_target_pairs={{0,6},{2,4},{4,2},{6,0},{1,7},{3,5},{5,3},{7,1},{8,14},{10,12},{12... | collective-permute-start | bytes 122888 | tf_op jit(solution)/shard_map/ppermute | solution.py:201
  6.6 0.6 collective-permute-start
  7.2 1.4 %collective-permute-done.2.refs_3_ = bf16[16,1280]{1,0:T(8,128)(2,1)S(1)} collective-permute-done((bf16[16,1280]{1,0:T(8,128)(2,1)S(1)}, bf16[16,1280]{1,0:T(8,128)(2,1)S(1)}, u32[]{:S(2)}, u32[]{:S(2)}) %collective-permute-start.2) | collective-permute-done | bytes 40992 | tf_op jit(solution)/shard_map/ppermute | solution.py:201
  8.6 2.9 %collective-permute-done.1.refs_2_ = bf16[16,1280]{1,0:T(8,128)(2,1)S(1)} collective-permute-done((bf16[16,1280]{1,0:T(8,128)(2,1)S(1)}, bf16[16,1280]{1,0:T(8,128)(2,1)S(1)}, u32[]{:S(2)}, u32[]{:S(2)}) %collective-permute-start.1) | collective-permute-done | bytes 40992 | tf_op jit(solution)/shard_map/ppermute | solution.py:201
  11.5 2.5 %collective-permute-start.5 = (bf16[4,16,1280]{2,1,0:T(8,128)(2,1)S(1)}, bf16[4,16,1280]{2,1,0:T(8,128)(2,1)S(1)}, u32[]{:S(2)}, u32[]{:S(2)}) collective-permute-start(bf16[4,16,1280]{2,1,0:T(8,128)(2,1)S(1)} %stack.1._.refs_0_), channel_id=1, source_target_pairs={{0,24},{8,16},{16,8},{24,0},{1,25},{9,17},{17,9},{25,1},{2,26},{10... | collective-permute-start | bytes 491528 | tf_op jit(solution)/shard_map/ppermute | solution.py:201
  14.0 0.5 collective-permute-start.4
  14.5 0.5 collective-permute-start.3
  15.1 10.6 %load.1 = (f32[2048,1024]{1,0:T(8,128)S(1)}, f32[2048,1024]{1,0:T(8,128)S(1)}, f32[2048,1024]{1,0:T(8,128)S(1)}, f32[2048,1024]{1,0:T(8,128)S(1)}) custom-call(bf16[4,16,1280]{2,1,0:T(8,128)(2,1)S(1)} %stack.1._.refs_0_, f32[8192,1024]{1,0:T(8,128)} %c_hbm.1), custom_call_target="tpu_custom_call" | custom-call | bytes 33554432 | tf_op jit(solution)/shard_map/load/pallas_call | solution.py:225
  25.7 0.6 collective-permute-start.7
  26.3 0.4 collective-permute-start.9
  26.8 0.5 collective-permute-done.7.refs_5_
  27.3 0.4 collective-permute-done.8.refs_6_
  27.9 1.8 %order.1 = (bf16[640,1024]{1,0:T(8,128)(2,1)S(1)}, s32[1]{0:T(128)}) custom-call(bf16[4,16,1280]{2,1,0:T(8,128)(2,1)S(1)} %stack.1._.refs_0_, bf16[4,16,1280]{2,1,0:T(8,128)(2,1)S(1)} %collective-permute-done.3.refs_1_, bf16[4,16,1280]{2,1,0:T(8,128)(2,1)S(1)} %collective-permute-done.4.refs_2_, bf16[4,16,1280]{2,1,0:T(8,128)(2,1)S(1)} %collective-permute-done.5.refs_3_, ...), custom_call_target="tpu_custom_call" | custom-call | tf_op jit(solution)/shard_map/order/pallas_call | solution.py:253
  29.7 16.1 %scores.1 = (bf16[2048,640]{1,0:T(8,128)(2,1)S(1)}, bf16[2048,640]{1,0:T(8,128)(2,1)S(1)}, bf16[2048,640]{1,0:T(8,128)(2,1)S(1)}, bf16[2048,640]{1,0:T(8,128)(2,...) custom-call(f32[2048,1024]{1,0:T(8,128)S(1)} %get-tuple-element.29.refs_0_, ...), custom_call_target="tpu_custom_call" | custom-call | tf_op jit(solution)/shard_map/scores/pallas_call | solution.py:270
  46.2 0.8 %collective-permute-done.10 = f32[8,640]{1,0:T(8,128)S(1)} collective-permute-done((f32[8,640]{1,0:T(8,128)S(1)}, f32[8,640]{1,0:T(8,128)S(1)}, u32[]{:S(2)}, u32[]{:S(2)}) %collective-permute-start.10) | collective-permute-done | bytes 20512 | tf_op jit(solution)/shard_map/ppermute | solution.py:201
  47.1 2.5 %collective-permute-start.13 = (f32[8,640]{1,0:T(8,128)S(1)}, f32[8,640]{1,0:T(8,128)S(1)}, u32[]{:S(2)}, u32[]{:S(2)}) collective-permute-start(f32[8,640]{1,0:T(8,128)S(1)} %maximum_maximum_fusion.refs_11_), channel_id=1, source_target_pairs={{0,24},{8,16},{16,8},{24,0},{1,25},{9,17},{17,9},{25,1},{2,26},{10... | collective-permute-start | bytes 61448 | tf_op jit(solution)/shard_map/ppermute | solution.py:201
  49.6 0.5 collective-permute-start.12
  50.1 0.5 collective-permute-start.11
  50.6 1.2 %collective-permute-done.13.refs_14_ = f32[8,640]{1,0:T(8,128)S(1)} collective-permute-done((f32[8,640]{1,0:T(8,128)S(1)}, f32[8,640]{1,0:T(8,128)S(1)}, u32[]{:S(2)}, u32[]{:S(2)}) %collective-permute-start.13) | collective-permute-done | bytes 20512 | tf_op jit(solution)/shard_map/ppermute | solution.py:201
  51.8 1.6 %collective-permute-done.12.refs_13_ = f32[8,640]{1,0:T(8,128)S(1)} collective-permute-done((f32[8,640]{1,0:T(8,128)S(1)}, f32[8,640]{1,0:T(8,128)S(1)}, u32[]{:S(2)}, u32[]{:S(2)}) %collective-permute-start.12) | collective-permute-done | bytes 20512 | tf_op jit(solution)/shard_map/ppermute | solution.py:201
  53.4 0.5 collective-permute-done.11.refs_12_
  53.9 15.7 %refresh.1 = (f32[2048,1024]{1,0:T(8,128)S(1)}, f32[2048,1024]{1,0:T(8,128)S(1)}, f32[2048,1024]{1,0:T(8,128)S(1)}, f32[2048,1024]{1,0:T(8,128)S(1)}, f32[8192,1024]{1,0:T(8,128)}) custom-call(f32[2048,1024]{1,0:T(8,128)S(1)} %get-tuple-element.29.refs_0_, ...), custom_call_target="tpu_custom_call", output_to_operand_aliasing={{0}: (0, {}), {1}: (1, {}), {2}: (2, {}), {3}: (3, {})} | custom-call | tf_op jit(solution)/shard_map/refresh/pallas_call | solution.py:292
  (18 shorter events, 0.9 us)
Async XLA Ops:
  0.0 0.8 %copy-start = (bf16[24,1024]{1,0:T(8,128)(2,1)S(1)}, bf16[24,1024]{1,0:T(8,128)(2,1)}, u32[]{:S(2)}) copy-start(bf16[24,1024]{1,0:T(8,128)(2,1)} %lat_ref.1) | copy-start | bytes 147460
  0.8 0.7 copy-start.1
  1.5 7.1 %collective-permute-start.2 = (bf16[16,1280]{1,0:T(8,128)(2,1)S(1)}, bf16[16,1280]{1,0:T(8,128)(2,1)S(1)}, u32[]{:S(2)}, u32[]{:S(2)}) collective-permute-start(bf16[16,1280]{1,0:T(8,128)(2,1)S(1)} %pack.1.refs_0_), channel_id=1, source_target_pairs={{0,6},{2,4},{4,2},{6,0},{1,7},{3,5},{5,3},{7,1},{8,14},{10,12},{12... | collective-permute-start | bytes 122888 | tf_op jit(solution)/shard_map/ppermute | solution.py:201
  6.6 4.9 %collective-permute-start.1 = (bf16[16,1280]{1,0:T(8,128)(2,1)S(1)}, bf16[16,1280]{1,0:T(8,128)(2,1)S(1)}, u32[]{:S(2)}, u32[]{:S(2)}) collective-permute-start(bf16[16,1280]{1,0:T(8,128)(2,1)S(1)} %pack.1.refs_0_), channel_id=1, source_target_pairs={{0,4},{2,6},{4,0},{6,2},{1,5},{3,7},{5,1},{7,3},{8,12},{10,14},{12... | collective-permute-start | bytes 122888 | tf_op jit(solution)/shard_map/ppermute | solution.py:201
  6.6 4.9 %collective-permute-start = (bf16[16,1280]{1,0:T(8,128)(2,1)S(1)}, bf16[16,1280]{1,0:T(8,128)(2,1)S(1)}, u32[]{:S(2)}, u32[]{:S(2)}) collective-permute-start(bf16[16,1280]{1,0:T(8,128)(2,1)S(1)} %pack.1.refs_0_), channel_id=1, source_target_pairs={{0,2},{2,0},{4,6},{6,4},{1,3},{3,1},{5,7},{7,5},{8,10},{10,8},{12,... | collective-permute-start | bytes 122888 | tf_op jit(solution)/shard_map/ppermute | solution.py:201
  11.5 14.1 %collective-permute-start.5 = (bf16[4,16,1280]{2,1,0:T(8,128)(2,1)S(1)}, bf16[4,16,1280]{2,1,0:T(8,128)(2,1)S(1)}, u32[]{:S(2)}, u32[]{:S(2)}) collective-permute-start(bf16[4,16,1280]{2,1,0:T(8,128)(2,1)S(1)} %stack.1._.refs_0_), channel_id=1, source_target_pairs={{0,24},{8,16},{16,8},{24,0},{1,25},{9,17},{17,9},{25,1},{2,26},{10... | collective-permute-start | bytes 491528 | tf_op jit(solution)/shard_map/ppermute | solution.py:201
  14.0 11.6 %collective-permute-start.4 = (bf16[4,16,1280]{2,1,0:T(8,128)(2,1)S(1)}, bf16[4,16,1280]{2,1,0:T(8,128)(2,1)S(1)}, u32[]{:S(2)}, u32[]{:S(2)}) collective-permute-start(bf16[4,16,1280]{2,1,0:T(8,128)(2,1)S(1)} %stack.1._.refs_0_), channel_id=1, source_target_pairs={{0,16},{8,24},{16,0},{24,8},{1,17},{9,25},{17,1},{25,9},{2,18},{10... | collective-permute-start | bytes 491528 | tf_op jit(solution)/shard_map/ppermute | solution.py:201
  14.5 11.1 %collective-permute-start.3 = (bf16[4,16,1280]{2,1,0:T(8,128)(2,1)S(1)}, bf16[4,16,1280]{2,1,0:T(8,128)(2,1)S(1)}, u32[]{:S(2)}, u32[]{:S(2)}) collective-permute-start(bf16[4,16,1280]{2,1,0:T(8,128)(2,1)S(1)} %stack.1._.refs_0_), channel_id=1, source_target_pairs={{0,8},{8,0},{16,24},{24,16},{1,9},{9,1},{17,25},{25,17},{2,10},{10... | collective-permute-start | bytes 491528 | tf_op jit(solution)/shard_map/ppermute | solution.py:201
  15.1 11.7 %collective-permute-start.6 = (bf16[4,16,1280]{2,1,0:T(8,128)(2,1)S(1)}, bf16[4,16,1280]{2,1,0:T(8,128)(2,1)S(1)}, u32[]{:S(2)}, u32[]{:S(2)}) collective-permute-start(bf16[4,16,1280]{2,1,0:T(8,128)(2,1)S(1)} %stack.1._.refs_0_), channel_id=1, source_target_pairs={{0,1},{1,0},{2,3},{3,2},{4,5},{5,4},{6,7},{7,6},{8,9},{9,8},{10,11... | collective-permute-start | bytes 491528 | tf_op jit(solution)/shard_map/ppermute | solution.py:201
  25.7 1.6 %collective-permute-start.7 = (bf16[4,16,1280]{2,1,0:T(8,128)(2,1)S(1)}, bf16[4,16,1280]{2,1,0:T(8,128)(2,1)S(1)}, u32[]{:S(2)}, u32[]{:S(2)}) collective-permute-start(bf16[4,16,1280]{2,1,0:T(8,128)(2,1)S(1)} %collective-permute-done.3.refs_1_), channel_id=1, source_target_pairs={{0,1},{1,0},{2,3},{3,2},{4,5},{5,4},{6,7},{7,6},{8,9},{9,8},{10,11... | collective-permute-start | bytes 491528 | tf_op jit(solution)/shard_map/ppermute | solution.py:201
  26.3 1.4 %collective-permute-start.8 = (bf16[4,16,1280]{2,1,0:T(8,128)(2,1)S(1)}, bf16[4,16,1280]{2,1,0:T(8,128)(2,1)S(1)}, u32[]{:S(2)}, u32[]{:S(2)}) collective-permute-start(bf16[4,16,1280]{2,1,0:T(8,128)(2,1)S(1)} %collective-permute-done.4.refs_2_), channel_id=1, source_target_pairs={{0,1},{1,0},{2,3},{3,2},{4,5},{5,4},{6,7},{7,6},{8,9},{9,8},{10,11... | collective-permute-start | bytes 491528 | tf_op jit(solution)/shard_map/ppermute | solution.py:201
  26.3 1.6 %collective-permute-start.9 = (bf16[4,16,1280]{2,1,0:T(8,128)(2,1)S(1)}, bf16[4,16,1280]{2,1,0:T(8,128)(2,1)S(1)}, u32[]{:S(2)}, u32[]{:S(2)}) collective-permute-start(bf16[4,16,1280]{2,1,0:T(8,128)(2,1)S(1)} %collective-permute-done.5.refs_3_), channel_id=1, source_target_pairs={{0,1},{1,0},{2,3},{3,2},{4,5},{5,4},{6,7},{7,6},{8,9},{9,8},{10,11... | collective-permute-start | bytes 491528 | tf_op jit(solution)/shard_map/ppermute | solution.py:201
  45.8 1.3 %collective-permute-start.10 = (f32[8,640]{1,0:T(8,128)S(1)}, f32[8,640]{1,0:T(8,128)S(1)}, u32[]{:S(2)}, u32[]{:S(2)}) collective-permute-start(f32[8,640]{1,0:T(8,128)S(1)} %get-tuple-element.43), channel_id=1, source_target_pairs={{0,1},{1,0},{2,3},{3,2},{4,5},{5,4},{6,7},{7,6},{8,9},{9,8},{10,11... | collective-permute-start | bytes 61448 | tf_op jit(solution)/shard_map/ppermute | solution.py:201
  47.1 4.7 %collective-permute-start.13 = (f32[8,640]{1,0:T(8,128)S(1)}, f32[8,640]{1,0:T(8,128)S(1)}, u32[]{:S(2)}, u32[]{:S(2)}) collective-permute-start(f32[8,640]{1,0:T(8,128)S(1)} %maximum_maximum_fusion.refs_11_), channel_id=1, source_target_pairs={{0,24},{8,16},{16,8},{24,0},{1,25},{9,17},{17,9},{25,1},{2,26},{10... | collective-permute-start | bytes 61448 | tf_op jit(solution)/shard_map/ppermute | solution.py:201
  49.6 3.8 %collective-permute-start.12 = (f32[8,640]{1,0:T(8,128)S(1)}, f32[8,640]{1,0:T(8,128)S(1)}, u32[]{:S(2)}, u32[]{:S(2)}) collective-permute-start(f32[8,640]{1,0:T(8,128)S(1)} %maximum_maximum_fusion.refs_11_), channel_id=1, source_target_pairs={{0,16},{8,24},{16,0},{24,8},{1,17},{9,25},{17,1},{25,9},{2,18},{10... | collective-permute-start | bytes 61448 | tf_op jit(solution)/shard_map/ppermute | solution.py:201
  50.1 3.8 %collective-permute-start.11 = (f32[8,640]{1,0:T(8,128)S(1)}, f32[8,640]{1,0:T(8,128)S(1)}, u32[]{:S(2)}, u32[]{:S(2)}) collective-permute-start(f32[8,640]{1,0:T(8,128)S(1)} %maximum_maximum_fusion.refs_11_), channel_id=1, source_target_pairs={{0,8},{8,0},{16,24},{24,16},{1,9},{9,1},{17,25},{25,17},{2,10},{10... | collective-permute-start | bytes 61448 | tf_op jit(solution)/shard_map/ppermute | solution.py:201
